TPU v7x, 128 devices: a whole 4x4x4 slice. The times are simulated.
128 devices in a mesh: ctx: 16 (over y_lo, z, core), mp: 8 (over y_hi, x).
Axes of the slice: x: 4, y: 4 (y_hi: 2, y_lo: 2; y = y_hi * 2 + y_lo), z: 4, core: 2. Of those that a mesh axis runs over, the one named last changes fastest.
Arguments:
- residual_in: bfloat16 [4, 32, 128, 1024], P(None, 'ctx', 'mp'), may hold values from -54 to 54
- attn_norm: float32 [1024], replicated, may hold values from 0.1 to 1.9
- query_key_value_weight: bfloat16 [1024, 8, 256], P(None, 'mp'), may hold values from -0.1875 to 0.1875
- query_gain: float32 [64], replicated, may hold values from 0.1 to 1.9
- key_gain: float32 [64], replicated, may hold values from 0.1 to 1.9
- out_weight: bfloat16 [1024, 1024], P('mp'), may hold values from -2 to 2
- ffn_norm: float32 [1024], replicated, may hold values from 0.1 to 1.9
- gate_up: bfloat16 [1024, 2, 4608], P(None, None, 'mp'), may hold values from -0.1875 to 0.1875
- down_weight: bfloat16 [4608, 1024], P('mp'), may hold values from -0.09375 to 0.09375
- cotangent: bfloat16 [4, 32, 128, 1024], P(None, 'ctx', 'mp'), may hold values from -6 to 6
- positions: int32 [4, 4096], replicated, may hold values from 256 to 8446, as said below
- block_map: int32 [32], replicated, may hold values from 0 to 31, as said below
Outputs:
- output: bfloat16 [4, 32, 128, 1024], P(None, 'ctx', 'mp')
- input_grad: bfloat16 [4, 32, 128, 1024], P(None, 'ctx', 'mp')
- attn_norm_grad: float32 [1024], replicated
- qkv_grad: float32 [1024, 8, 256], P(None, 'mp')
- query_gain_grad: float32 [64], replicated
- key_gain_grad: float32 [64], replicated
- out_grad: float32 [1024, 1024], P('mp')
- ffn_norm_grad: float32 [1024], replicated
- gate_up_grad: float32 [1024, 2, 4608], P(None, None, 'mp')
- down_grad: float32 [4608, 1024], P('mp')
Inputs may be any that keep to these rules, and one draw needn't show every extreme that they name: `positions`: positions rise strictly along each sequence in steps of 1 or 2; every sequence ends at 8446. `block_map`: each block of a sequence stands in exactly one slot; slots 2c and 2c + 1 hold blocks b and 31 - b for some b, in either order.
All inputs are finite; a program needn't handle non-finite values.
Results may differ from a plain program's by a relative error of at most 0.028.
Values may be sent and summed in bfloat16 or wider, within the bound.
A program may use at most 128 MiB of HBM per device.

v0:
```python
import math

import jax
import jax.numpy as jnp
from jax import lax
from jax.sharding import PartitionSpec as P

EPSILON = 1e-05
ROPE_BASE = 1000000.0


def cut_along(array, dim, length):
    dims = array.shape
    pieces = array.reshape(*dims[:dim], length, dims[dim] // length, *dims[dim + 1 :])
    return jnp.moveaxis(pieces, dim, 0)


def summed_on_arrival(array, axis, dim):
    pieces = cut_along(array, dim, lax.axis_size(axis))
    arrived = lax.all_to_all(pieces, axis, split_axis=0, concat_axis=0, tiled=True)
    return arrived.astype(jnp.float32).sum(axis=0)


def together(arrays, axis):
    ends = [0]
    for a in arrays:
        ends.append(ends[-1] + a.size)
    so_far = lax.psum(jnp.concatenate([a.ravel() for a in arrays]), axis)
    return tuple((so_far[b:e].reshape(a.shape) for a, b, e in zip(arrays, ends, ends[1:])))


def rms_scale(values):
    return lax.rsqrt(jnp.mean(values * values, axis=-1, keepdims=True) + EPSILON)


def rotate(values, cosine_table, sine_table):
    half_dim = values.shape[-1] // 2
    first_half = values[..., :half_dim]
    second_half = values[..., half_dim:]
    return jnp.concatenate(
        [
            first_half * cosine_table - second_half * sine_table,
            second_half * cosine_table + first_half * sine_table,
        ],
        axis=-1,
    )


def rotate_back(gradient, cosine_table, sine_table):
    half_dim = gradient.shape[-1] // 2
    first_half = gradient[..., :half_dim]
    second_half = gradient[..., half_dim:]
    return jnp.concatenate(
        [
            first_half * cosine_table + second_half * sine_table,
            second_half * cosine_table - first_half * sine_table,
        ],
        axis=-1,
    )


def norm_back(gradient, normed, scale_rows, gain_vec):
    scaled = gradient * gain_vec
    return scale_rows * (scaled - normed * jnp.mean(scaled * normed, axis=-1, keepdims=True))


def local(
    residual_in,
    attn_norm,
    query_key_value_weight,
    query_gain,
    key_gain,
    out_weight,
    ffn_norm,
    gate_up,
    down_weight,
    cotangent,
    positions,
    block_map,
):
    mp_size = lax.axis_size("mp")
    ctx_size = lax.axis_size("ctx")
    ctx_index = lax.axis_index("ctx")
    sequences, slot_pair, rows_per_block, width = residual_in.shape
    row_count = sequences * slot_pair * rows_per_block
    block_len = rows_per_block * mp_size
    local_len = slot_pair * block_len
    slot_count = slot_pair * ctx_size
    head_dim = query_gain.shape[0]
    kv_local = query_key_value_weight.shape[1]
    group_size = query_key_value_weight.shape[2] // head_dim - 2
    ff_local = gate_up.shape[2]
    query_rows = group_size * local_len
    scale_factor = 1.0 / math.sqrt(head_dim)
    span_slots = max(1, min(slot_count, 512 // block_len))
    while slot_count % span_slots:
        span_slots = span_slots - 1
    group_count = slot_count // span_slots
    kv_cols = kv_local * 2 * head_dim

    def to_sequence(row_array):
        columns = row_array.shape[-1]
        shaped = row_array.reshape(mp_size, sequences, slot_pair, rows_per_block, columns)
        return shaped.transpose(1, 2, 0, 3, 4).reshape(sequences, local_len, columns)

    def to_rows(seq_array):
        columns = seq_array.shape[-1]
        shaped = seq_array.reshape(sequences, slot_pair, mp_size, rows_per_block, columns)
        return shaped.transpose(2, 0, 1, 3, 4).reshape(mp_size * row_count, columns)

    tokens = residual_in.reshape(row_count, width).astype(jnp.float32)
    scale_one = rms_scale(tokens)
    tokens_normed = tokens * scale_one
    full_one = lax.all_gather(
        (tokens_normed * attn_norm).astype(jnp.bfloat16), "mp", axis=0, tiled=True
    )
    qkv_flat = query_key_value_weight.reshape(width, -1)
    query_key_value_rows = jnp.dot(full_one, qkv_flat, preferred_element_type=jnp.float32)
    query_key_value_rows = to_sequence(query_key_value_rows).reshape(
        sequences, local_len, kv_local, group_size + 2, head_dim
    )
    own_blocks = lax.dynamic_slice_in_dim(block_map, ctx_index * slot_pair, slot_pair)
    row_iota = jnp.arange(block_len, dtype=jnp.int32)
    query_index = (own_blocks[:, None] * block_len + row_iota[None, :]).reshape(local_len)
    inverse_freq = 1.0 / ROPE_BASE ** (jnp.arange(0, head_dim, 2, dtype=jnp.float32) / head_dim)
    angles = jnp.take(positions, query_index, axis=1).astype(jnp.float32)[:, :, None] * inverse_freq
    cosine_table = jnp.cos(angles)
    sine_table = jnp.sin(angles)
    cosine_query = cosine_table[:, :, None, None, :]
    sine_query = sine_table[:, :, None, None, :]
    cosine_key = cosine_table[:, :, None, :]
    sine_key = sine_table[:, :, None, :]
    query_raw = query_key_value_rows[:, :, :, :group_size]
    key_raw = query_key_value_rows[:, :, :, group_size]
    value_raw = query_key_value_rows[:, :, :, group_size + 1]
    query_scale = rms_scale(query_raw)
    query_normed = query_raw * query_scale
    key_scale = rms_scale(key_raw)
    key_normed = key_raw * key_scale
    query_matrix = rotate(query_normed * query_gain, cosine_query, sine_query).astype(jnp.bfloat16)
    key_rows = rotate(key_normed * key_gain, cosine_key, sine_key).astype(jnp.bfloat16)
    values = value_raw.astype(jnp.bfloat16)
    query_mat = query_matrix.transpose(0, 2, 3, 1, 4).reshape(
        sequences, kv_local, query_rows, head_dim
    )
    query_order = jnp.tile(query_index, group_size)
    latest = jnp.max(query_index)
    kv_pack = jnp.stack([key_rows, values], axis=3).reshape(
        sequences, slot_pair, block_len, kv_cols
    )
    kv_every = lax.all_gather(kv_pack, "ctx", axis=1, tiled=True)

    def key_slots(start_slot, count):
        packed = lax.dynamic_slice_in_dim(kv_every, start_slot, count, 1)
        packed = packed.reshape(sequences, count * block_len, kv_local, 2, head_dim).transpose(
            0, 2, 1, 3, 4
        )
        block_ids = lax.dynamic_slice_in_dim(block_map, start_slot, count)
        key_index = (block_ids[:, None] * block_len + row_iota[None, :]).reshape(-1)
        return (packed[..., 0, :], packed[..., 1, :], key_index)

    def scores_of(key_block, key_index):
        scores = (
            jnp.einsum("shqd,shkd->shqk", query_mat, key_block, preferred_element_type=jnp.float32)
            * scale_factor
        )
        allowed = key_index[None, :] <= query_order[:, None]
        return (scores, allowed)

    row_shape = (sequences, kv_local, query_rows)

    def stats_step(group_index, loop_state):
        key_block, value_block, key_index = key_slots(group_index * span_slots, span_slots)

        def stats_update(state_now):
            running_max, running_sum = state_now
            scores, allowed = scores_of(key_block, key_index)
            new_max = jnp.maximum(running_max, jnp.max(jnp.where(allowed, scores, -1e30), axis=-1))
            weights = jnp.where(allowed, jnp.exp(scores - new_max[..., None]), 0.0)
            return (
                new_max,
                running_sum * jnp.exp(running_max - new_max) + jnp.sum(weights, axis=-1),
            )

        return lax.cond(
            jnp.min(key_index) <= latest, stats_update, lambda state_now: state_now, loop_state
        )

    running_max, running_sum = lax.fori_loop(
        0,
        group_count,
        stats_step,
        (jnp.full(row_shape, -1e30, jnp.float32), jnp.zeros(row_shape, jnp.float32)),
    )
    log_total = running_max + jnp.log(running_sum)

    def probs_of(key_block, key_index):
        scores, allowed = scores_of(key_block, key_index)
        return jnp.where(allowed, jnp.exp(scores - log_total[..., None]), 0.0)

    def output_step(group_index, loop_state):
        key_block, value_block, key_index = key_slots(group_index * span_slots, span_slots)

        def output_update(state_now):
            weights = probs_of(key_block, key_index).astype(jnp.bfloat16)
            return state_now + jnp.einsum(
                "shqk,shkd->shqd", weights, value_block, preferred_element_type=jnp.float32
            )

        return lax.cond(
            jnp.min(key_index) <= latest, output_update, lambda state_now: state_now, loop_state
        )

    attended = lax.fori_loop(
        0, group_count, output_step, jnp.zeros(row_shape + (head_dim,), jnp.float32)
    )
    attended_low = attended.astype(jnp.bfloat16)
    attended_rows = to_rows(
        attended_low.reshape(sequences, kv_local, group_size, local_len, head_dim)
        .transpose(0, 3, 1, 2, 4)
        .reshape(sequences, local_len, kv_local * group_size * head_dim)
    )
    mixed_rows = tokens + lax.psum_scatter(
        jnp.dot(attended_rows, out_weight, preferred_element_type=jnp.float32).astype(jnp.bfloat16),
        "mp",
        scatter_dimension=0,
        tiled=True,
    ).astype(jnp.float32)
    scale_two = rms_scale(mixed_rows)
    mixed_normed = mixed_rows * scale_two
    full_two = lax.all_gather(
        (mixed_normed * ffn_norm).astype(jnp.bfloat16), "mp", axis=0, tiled=True
    )
    gate_up_flat = gate_up.reshape(width, 2 * ff_local)
    gate_values = jnp.dot(full_two, gate_up_flat, preferred_element_type=jnp.float32)
    gate_part = gate_values[:, :ff_local]
    up_values = gate_values[:, ff_local:]
    sigmoid_gate = jax.nn.sigmoid(gate_part)
    active = (gate_part * sigmoid_gate * up_values).astype(jnp.bfloat16)
    output = (
        (
            mixed_rows
            + summed_on_arrival(
                jnp.dot(active, down_weight, preferred_element_type=jnp.float32).astype(
                    jnp.bfloat16
                ),
                "mp",
                0,
            )
        )
        .astype(jnp.bfloat16)
        .reshape(residual_in.shape)
    )
    grad_output = cotangent.reshape(row_count, width)
    grad_full = lax.all_gather(grad_output, "mp", axis=0, tiled=True)
    down_grad = jnp.einsum("rf,rd->fd", active, grad_full, preferred_element_type=jnp.float32)
    grad_active = jnp.einsum(
        "rd,fd->rf", grad_full, down_weight, preferred_element_type=jnp.float32
    )
    grad_gate = grad_active * up_values * sigmoid_gate * (1.0 + gate_part * (1.0 - sigmoid_gate))
    grad_up = grad_active * gate_part * sigmoid_gate
    grad_gate_up = jnp.concatenate([grad_gate, grad_up], axis=1).astype(jnp.bfloat16)
    gate_up_grad = jnp.einsum(
        "rd,rf->df", full_two, grad_gate_up, preferred_element_type=jnp.float32
    ).reshape(width, 2, ff_local)
    gate_up_grad, down_grad = (
        lax.psum(gate_up_grad.astype(jnp.bfloat16), "ctx").astype(jnp.float32),
        lax.psum(down_grad.astype(jnp.bfloat16), "ctx").astype(jnp.float32),
    )
    grad_normed_two = summed_on_arrival(
        jnp.einsum(
            "rf,df->rd", grad_gate_up, gate_up_flat, preferred_element_type=jnp.float32
        ).astype(jnp.bfloat16),
        "mp",
        0,
    )
    ffn_norm_part = jnp.sum(grad_normed_two * mixed_normed, axis=0)
    grad_mixed = grad_output.astype(jnp.float32) + norm_back(
        grad_normed_two, mixed_normed, scale_two, ffn_norm
    )
    grad_mixed_full = lax.all_gather(grad_mixed.astype(jnp.bfloat16), "mp", axis=0, tiled=True)
    out_grad = jnp.einsum(
        "rc,rd->cd", attended_rows, grad_mixed_full, preferred_element_type=jnp.float32
    )
    grad_attended = jnp.einsum(
        "rd,cd->rc", grad_mixed_full, out_weight, preferred_element_type=jnp.float32
    ).astype(jnp.bfloat16)
    grad_attended = to_sequence(grad_attended).reshape(
        sequences, local_len, kv_local, group_size, head_dim
    )
    grad_attended = grad_attended.transpose(0, 2, 3, 1, 4).reshape(
        sequences, kv_local, query_rows, head_dim
    )
    row_delta = jnp.sum(grad_attended.astype(jnp.float32) * attended, axis=-1)

    def back_piece(start_slot, count, grad_query):
        key_block, value_block, key_index = key_slots(start_slot, count)
        prob_block = probs_of(key_block, key_index)
        grad_probs = jnp.einsum(
            "shqd,shkd->shqk", grad_attended, value_block, preferred_element_type=jnp.float32
        )
        grad_scores = (prob_block * (grad_probs - row_delta[..., None])).astype(jnp.bfloat16)
        grad_query = (
            grad_query
            + jnp.einsum(
                "shqk,shkd->shqd", grad_scores, key_block, preferred_element_type=jnp.float32
            )
            * scale_factor
        )
        grad_key = (
            jnp.einsum(
                "shqk,shqd->shkd", grad_scores, query_mat, preferred_element_type=jnp.float32
            )
            * scale_factor
        )
        grad_value = jnp.einsum(
            "shqk,shqd->shkd",
            prob_block.astype(jnp.bfloat16),
            grad_attended,
            preferred_element_type=jnp.float32,
        )
        piece_grads = jnp.stack([grad_key, grad_value], axis=3).transpose(0, 2, 1, 3, 4)
        return (grad_query, piece_grads.reshape(sequences, count, block_len, kv_cols), key_index)

    query_zero = jnp.zeros(row_shape + (head_dim,), jnp.float32)

    def back_step(group_index, loop_state):
        block_ids = lax.dynamic_slice_in_dim(block_map, group_index * span_slots, span_slots)
        least = jnp.min(block_ids) * block_len

        def back_update(state_now):
            query_now, grad_pack = state_now
            query_now, piece_grads, key_index = back_piece(
                group_index * span_slots, span_slots, query_now
            )
            grad_pack = lax.dynamic_update_slice_in_dim(
                grad_pack, piece_grads, group_index * span_slots, 1
            )
            return (query_now, grad_pack)

        return lax.cond(least <= latest, back_update, lambda state_now: state_now, loop_state)

    grad_query, grad_pack = lax.fori_loop(
        0,
        group_count,
        back_step,
        (query_zero, jnp.zeros((sequences, slot_count, block_len, kv_cols), jnp.float32)),
    )
    grad_kv_own = (
        lax.psum_scatter(grad_pack.astype(jnp.bfloat16), "ctx", scatter_dimension=1, tiled=True)
        .astype(jnp.float32)
        .reshape(sequences, local_len, kv_local, 2, head_dim)
    )
    grad_query = grad_query.reshape(sequences, kv_local, group_size, local_len, head_dim).transpose(
        0, 3, 1, 2, 4
    )
    grad_query_turned = rotate_back(grad_query, cosine_query, sine_query)
    grad_key_turned = rotate_back(grad_kv_own[:, :, :, 0, :], cosine_key, sine_key)
    query_gain_part = jnp.sum(grad_query_turned * query_normed, axis=(0, 1, 2, 3))
    key_gain_part = jnp.sum(grad_key_turned * key_normed, axis=(0, 1, 2))
    grad_qkv = jnp.concatenate(
        [
            norm_back(grad_query_turned, query_normed, query_scale, query_gain),
            norm_back(grad_key_turned, key_normed, key_scale, key_gain)[:, :, :, None, :],
            grad_kv_own[:, :, :, 1:2, :],
        ],
        axis=3,
    ).astype(jnp.bfloat16)
    grad_qkv_rows = to_rows(
        grad_qkv.reshape(sequences, local_len, kv_local * (group_size + 2) * head_dim)
    )
    qkv_grad = jnp.einsum(
        "rd,rc->dc", full_one, grad_qkv_rows, preferred_element_type=jnp.float32
    ).reshape(query_key_value_weight.shape)
    grad_normed_one = summed_on_arrival(
        jnp.einsum("rc,dc->rd", grad_qkv_rows, qkv_flat, preferred_element_type=jnp.float32).astype(
            jnp.bfloat16
        ),
        "mp",
        0,
    )
    attn_norm_part = jnp.sum(grad_normed_one * tokens_normed, axis=0)
    input_grad = (
        (grad_mixed + norm_back(grad_normed_one, tokens_normed, scale_one, attn_norm))
        .astype(jnp.bfloat16)
        .reshape(residual_in.shape)
    )
    qkv_grad, out_grad = tuple(
        (
            part.astype(jnp.float32)
            for part in together(
                (qkv_grad.astype(jnp.bfloat16), out_grad.astype(jnp.bfloat16)), "ctx"
            )
        )
    )
    gain_sums = lax.psum(
        (attn_norm_part, ffn_norm_part, query_gain_part, key_gain_part), ("ctx", "mp")
    )
    return (
        output,
        input_grad,
        gain_sums[0],
        qkv_grad,
        gain_sums[2],
        gain_sums[3],
        out_grad,
        gain_sums[1],
        gate_up_grad,
        down_grad,
    )


def solution(mesh):
    return jax.shard_map(
        local,
        mesh=mesh,
        in_specs=(
            P(None, "ctx", "mp", None),
            P(),
            P(None, "mp", None),
            P(),
            P(),
            P("mp", None),
            P(),
            P(None, None, "mp"),
            P("mp", None),
            P(None, "ctx", "mp", None),
            P(),
            P(),
        ),
        out_specs=(
            P(None, "ctx", "mp", None),
            P(None, "ctx", "mp", None),
            P(),
            P(None, "mp", None),
            P(),
            P(),
            P("mp", None),
            P(),
            P(None, None, "mp"),
            P("mp", None),
        ),
        check_vma=False,
    )
```

profile of v0, /device:TPU:0, one launch (start us, length us, event | category | flops | bytes accessed | tf_op | source)
XLA Modules:
  0.0 905.1 jit_solution(16681900112490739695)
XLA Ops:
  16.7 51.7 %all-gather.6.cloned.1.call-done = bf16[1024,1024]{1,0:T(8,128)(2,1)} async-done(((bf16[128,1024]{1,0:T(8,128)(2,1)}), bf16[1024,1024]{1,0:T(8,128)(2,1)}) %all-gather.6.cloned.1.call-update) | async-done | bytes 2097168 | tf_op jit(solution)/shard_map/all_gather | solution.py:114
  93.8 25.8 %all-gather.8.cloned.1.call-done = bf16[4,32,128,128]{3,2,0,1:T(8,128)(2,1)} async-done(((bf16[4,2,128,128]{3,2,0,1:T(8,128)(2,1)}), bf16[4,32,128,128]{3,2,0,1:T(8,128)(2,1)}) %all-gather.8.cloned.1.call-update) | async-done | bytes 4194320 | tf_op jit(solution)/shard_map/all_gather | solution.py:151
  119.6 7.9 copy.180
  127.5 61.4 %while.49 = (s32[]{:T(128)}, f32[4,1,512]{2,0,1:T(4,128)S(1)}, f32[4,1,512]{2,0,1:T(4,128)S(1)}, s32[32]{0:T(128)S(1)}, s32[]{:T(128)}, /*index=5*/bf16[4,32,128...) while((s32[]{:T(128)}, f32[4,1,512]{2,0,1:T(4,128)S(1)}, ...), condition=%wide.region_10.11_spmd.clone, body=%wide.region_4.10_spmd.clone.sunk | while | flops 141825040 | bytes 11916621 | solution.py:189
  189.8 65.3 %while.50 = (s32[]{:T(128)}, f32[4,1,512,64]{2,3,0,1:T(8,128)}, s32[32]{0:T(128)S(1)}, s32[]{:T(128)}, bf16[4,32,128,128]{2,1,3,0:T(8,128)(2,1)}, /*index=5*/bf1...) while((s32[]{:T(128)}, f32[4,1,512,64]{2,3,0,1:T(8,128)}, ...), condition=%wide.region_15.16_spmd.clone, body=%wide.region_11.0_spmd.clone.sunk | while | flops 273024000 | bytes 4478253 | solution.py:214
  263.1 75.4 %reduce-scatter.3.cloned.1.call-done = bf16[128,1024]{1,0:T(8,128)(2,1)} async-done(((bf16[1024,1024]{1,0:T(8,128)(2,1)}), bf16[128,1024]{1,0:T(8,128)(2,1)}) %reduce-scatter.3.cloned.1.call-update) | async-done | bytes 262160 | tf_op jit(solution)/shard_map/reduce_scatter | solution.py:223
  342.3 53.0 %all-gather.10.cloned.1.call-done = bf16[1024,1024]{1,0:T(8,128)(2,1)} async-done(((bf16[128,1024]{1,0:T(8,128)(2,1)}), bf16[1024,1024]{1,0:T(8,128)(2,1)}) %all-gather.10.cloned.1.call-update) | async-done | bytes 2097168 | tf_op jit(solution)/shard_map/all_gather | solution.py:231
  402.0 49.6 %all-gather.12.cloned.1.call-done = bf16[1024,1024]{1,0:T(8,128)(2,1)} async-done(((bf16[128,1024]{1,0:T(8,128)(2,1)}), bf16[1024,1024]{1,0:T(8,128)(2,1)}) %all-gather.12.cloned.1.call-update) | async-done | bytes 2097168 | tf_op jit(solution)/shard_map/all_gather | solution.py:255
  461.7 30.0 %all_to_all.15 = bf16[8,128,1024]{2,1,0:T(8,128)(2,1)S(1)} all-to-all(bf16[8,128,1024]{2,1,0:T(8,128)(2,1)S(1)} %bitcast.307), channel_id=1, replica_groups=mesh['ctx'=16,'mp'=8] {'mp'}, dimensions={0} | all-to-all | bytes 4194304 | tf_op jit(solution)/shard_map/all_to_all | solution.py:20
  494.5 52.4 %all-gather.14.cloned.1.call-done = bf16[1024,1024]{1,0:T(8,128)(2,1)} async-done(((bf16[128,1024]{1,0:T(8,128)(2,1)}), bf16[1024,1024]{1,0:T(8,128)(2,1)}) %all-gather.14.cloned.1.call-update) | async-done | bytes 2097168 | tf_op jit(solution)/shard_map/all_gather | solution.py:281
  553.9 79.9 %while.51 = (s32[]{:T(128)}, f32[4,1,512,64]{2,3,0,1:T(8,128)S(1)}, bf16[4,32,128,128]{2,1,3,0:T(8,128)(2,1)}, s32[32]{0:T(128)S(1)}, s32[]{:T(128)}, /*index=5*...) while((s32[]{:T(128)}, f32[4,1,512,64]{2,3,0,1:T(8,128)S(1)}, ...), condition=%wide.region_26.27_spmd.clone, body=%wide.region_22.0_spmd.clone.sunk | while | flops 682623488 | bytes 29399528 | solution.py:343
  555.9 8.0 conditional.11
  565.9 8.0 conditional.11
  575.9 8.0 conditional.11
  585.9 8.0 conditional.11
  595.9 8.0 conditional.11
  605.8 8.0 conditional.11
  615.8 8.0 conditional.11
  625.8 8.0 conditional.11
  681.4 43.3 %reduce-scatter.5.cloned.1.call-done = bf16[4,2,128,128]{3,2,0,1:T(8,128)(2,1)} async-done(((bf16[4,32,128,128]{3,2,0,1:T(8,128)(2,1)}), bf16[4,2,128,128]{3,2,0,1:T(8,128)(2,1)}) %reduce-scatter.5.cloned.1.call-update) | async-done | bytes 262160 | tf_op jit(solution)/shard_map/reduce_scatter | solution.py:350
  737.4 9.4 %all-to-all-start.2 = ((bf16[8,128,1024]{2,1,0:T(8,128)(2,1)}), bf16[8,128,1024]{2,1,0:T(8,128)(2,1)S(1)}, u32[]{:S(2)}, u32[]{:S(2)}) async-start(bf16[8,128,1024]{2,1,0:T(8,128)(2,1)} %bitcast.296), calls=%async_computation.4 | async-start | bytes 4194304 | tf_op jit(solution)/shard_map/all_to_all | solution.py:20
  749.6 24.4 %all-to-all-done.2 = bf16[8,128,1024]{2,1,0:T(8,128)(2,1)S(1)} async-done(((bf16[8,128,1024]{2,1,0:T(8,128)(2,1)}), bf16[8,128,1024]{2,1,0:T(8,128)(2,1)S(1)}, u32[]{:S(2)}, u32[]{:S(2)}) %all-to-all-start.2) | async-done | bytes 2097184 | tf_op jit(solution)/shard_map/all_to_all | solution.py:20
  774.7 68.8 %all-reduce = (f32[1024]{0:T(1024)}, f32[64]{0:T(128)}, f32[64]{0:T(128)}, f32[1024]{0:T(1024)}) all-reduce(f32[1024]{0:T(1024)S(1)} %get-tuple-element.860, f32[64]{0:T(128)S(1)} %get-tuple-element.854, f32[64]{0:T(128)S(1)} %get-tuple-element.858, f32[1024]{0:T(1024)S(1)} %get-tuple-element.856), channel_id=1, replica_groups=mesh['ctx'=16,'mp'=8] {'ctx','mp'}, use_global_device_ids=true, to_apply=%region_33.34 | all-reduce | flops 2176 | bytes 17408 | tf_op jit(solution)/shard_map/psum | solution.py:396
  845.8 42.1 %all-reduce.4.cloned.1.call-done = (bf16[393216]{0:T(1024)(128)(2,1)}, bf16[1024,2,576]{0,2,1:T(8,128)(2,1)}, bf16[576,1024]{1,0:T(8,128)(2,1)}) async-done(((bf16[393216]{0:T(1024)(128)(2,1)}, bf16[1024,2,576]{0,2,1:T(8,128)(2,1)}, bf16[576,1024]{1,0:T(8,128)(2,1)}), (bf16[393216]{0:T(1024)(128)(2,1)}, bf16[1024,2,576]{0,2,1:T(8,128)(2,1)}, bf16[576,1024]{1,0:T(8,128)(2,1)})) %all-reduce.4.cloned.1.call-update) | async-done | bytes 4325392 | tf_op jit(solution)/shard_map/psum | solution.py:28
  (506 shorter events, 416.6 us)
Async XLA Ops:
  7.2 388.1 %copy-start = (bf16[1024,2,576]{0,2,1:T(8,128)(2,1)S(1)}, bf16[1024,2,576]{0,2,1:T(8,128)(2,1)}, u32[]{:S(2)}) copy-start(bf16[1024,2,576]{0,2,1:T(8,128)(2,1)} %param.31) | copy-start | bytes 7077892
  7.2 6.1 copy-start.29
  7.2 61.1 %copy-start.17 = (bf16[1024,1,256]{2,0,1:T(8,128)(2,1)S(1)}, bf16[1024,1,256]{2,0,1:T(8,128)(2,1)}, u32[]{:S(2)}) copy-start(bf16[1024,1,256]{2,0,1:T(8,128)(2,1)} %param.26) | copy-start | bytes 1572868
  7.2 61.1 %all-gather.6.cloned.1.call-start = ((), (), s32[]{:S(2)}) async-start(), calls=%async_computation.5 | async-start | bytes 2359296 | tf_op jit(solution)/shard_map/all_gather | solution.py:114
  10.4 109.2 %all-gather.8.cloned.1.call-start = ((), (), s32[]{:S(2)}) async-start(), calls=%async_computation.6 | async-start | bytes 4456448 | tf_op jit(solution)/shard_map/all_gather | solution.py:151
  74.8 6.7 copy-start.25
  81.4 6.9 copy-start.8
  82.2 6.1 copy-start.26
  83.1 255.3 %reduce-scatter.3.cloned.1.call-start = ((), (), s32[]{:S(2)}) async-start(), calls=%async_computation.7 | async-start | bytes 2359296 | tf_op jit(solution)/shard_map/reduce_scatter | solution.py:223
  255.0 6.0 copy-start.20
  261.0 77.5 %copy-start.4 = (bf16[4,2,16,1024]{3,2,1,0:T(8,128)(2,1)S(1)}, bf16[4,2,16,1024]{3,2,1,0:T(8,128)(2,1)}, u32[]{:S(2)}) copy-start(bf16[4,2,16,1024]{3,2,1,0:T(8,128)(2,1)} %param.24) | copy-start | bytes 786436
  261.0 78.6 %copy-start.23 = (f32[1024]{0:T(1024)S(1)}, f32[1024]{0:T(1024)}, u32[]{:S(2)}) copy-start(f32[1024]{0:T(1024)} %param.30) | copy-start | bytes 12292
  263.0 132.2 %all-gather.10.cloned.1.call-start = ((), (), s32[]{:S(2)}) async-start(), calls=%async_computation.8 | async-start | bytes 2359296 | tf_op jit(solution)/shard_map/all_gather | solution.py:231
  341.4 110.1 %all-gather.12.cloned.1.call-start = ((), (), s32[]{:S(2)}) async-start(), calls=%async_computation.9 | async-start | bytes 2359296 | tf_op jit(solution)/shard_map/all_gather | solution.py:255
  342.0 204.9 %all-gather.14.cloned.1.call-start = ((), (), s32[]{:S(2)}) async-start(), calls=%async_computation.10 | async-start | bytes 2359296 | tf_op jit(solution)/shard_map/all_gather | solution.py:281
  492.6 54.2 %copy-start.21 = (bf16[128,1024]{1,0:T(8,128)(2,1)S(1)}, bf16[128,1024]{1,0:T(8,128)(2,1)}, u32[]{:S(2)}) copy-start(bf16[128,1024]{1,0:T(8,128)(2,1)} %param.29) | copy-start | bytes 786436
  493.9 230.7 %reduce-scatter.5.cloned.1.call-start = ((), (), s32[]{:S(2)}) async-start(), calls=%async_computation.11 | async-start | bytes 4456448 | tf_op jit(solution)/shard_map/reduce_scatter | solution.py:350
  657.9 79.5 %all-to-all-start = ((bf16[8,128,1024]{2,1,0:T(8,128)(2,1)}), bf16[8,128,1024]{2,1,0:T(8,128)(2,1)}, u32[]{:S(2)}, u32[]{:S(2)}) async-start(bf16[8,128,1024]{2,1,0:T(8,128)(2,1)} %bitcast.45), calls=%async_computation.1 | async-start | bytes 4194304 | tf_op jit(solution)/shard_map/all_to_all | solution.py:20
  662.3 225.6 %all-reduce.4.cloned.1.call-start = ((), (), s32[]{:S(2)}) async-start(), calls=%async_computation.12 | async-start | bytes 8650752 | tf_op jit(solution)/shard_map/psum | solution.py:28
  681.3 45.2 %copy-start.9 = (f32[4,256,1,1,64]{1,4,0,3,2:T(8,128)S(1)}, f32[4,256,1,1,64]{1,4,0,3,2:T(8,128)}, u32[]{:S(2)}) copy-start(f32[4,256,1,1,64]{1,4,0,3,2:T(8,128)} %copy-done.8) | copy-start | bytes 786436
  681.3 46.3 %copy-start.16 = (bf16[4,256,1,2,64]{4,3,1,0,2:T(2,128)(2,1)S(1)}, bf16[4,256,1,2,64]{4,3,1,0,2:T(2,128)(2,1)}, u32[]{:S(2)}) copy-start(bf16[4,256,1,2,64]{4,3,1,0,2:T(2,128)(2,1)} %multiply_convert_fusion.3) | copy-start | bytes 786436
  737.4 36.6 %all-to-all-start.2 = ((bf16[8,128,1024]{2,1,0:T(8,128)(2,1)}), bf16[8,128,1024]{2,1,0:T(8,128)(2,1)S(1)}, u32[]{:S(2)}, u32[]{:S(2)}) async-start(bf16[8,128,1024]{2,1,0:T(8,128)(2,1)} %bitcast.296), calls=%async_computation.4 | async-start | bytes 4194304 | tf_op jit(solution)/shard_map/all_to_all | solution.py:20
  746.8 27.6 %copy-start.24 = (f32[1024]{0:T(1024)S(1)}, f32[1024]{0:T(1024)}, u32[]{:S(2)}) copy-start(f32[1024]{0:T(1024)} %param.25) | copy-start | bytes 12292
  891.9 6.2 copy-start.1
  (18 other events, 57.7 us)
Sparse Core Ops, SparseCore 0:
  11.0 57.3 all-gather.5
  83.3 36.2 all-gather.7
  263.2 75.2 reduce-scatter.2
  341.5 53.7 all-gather.9
  397.7 53.7 all-gather.11
  494.1 52.7 all-gather.13
  641.5 83.1 reduce-scatter.4
  734.5 153.4 all-reduce.3
where the time goes:
time: 915 us; the launch traced here: 905 us
  waiting for transfers between devices  418 us (46%)
  matrix products  122 us (13%)
  local copies, waits for them, and re-layouts  119 us (13%)
  blocking collectives  98.8 us (11%)
  other arithmetic  84.1 us (9%)
  loops' own time  33.1 us (4%)
  starting transfers between devices  14.9 us (2%)
  between operations  14.9 us (2%)
    reduce_scatter x1, waiting for transfers between devices, local(): lax.psum_scatter(jnp.dot(attended_rows, out_weight, preferred_element_typ...  75.4 us
    psum x1, blocking collectives, local(): lax.psum((attn_norm_part, ffn_norm_part, query_gain_part, key_gain_part),...  68.8 us
    all_gather x1, waiting for transfers between devices, local(): lax.all_gather((mixed_normed * ffn_norm).astype(jnp.bfloat16), 'mp', axis...  53 us
    all_gather x1, waiting for transfers between devices, local(): lax.all_gather(grad_mixed.astype(jnp.bfloat16), 'mp', axis=0, tiled=True)  52.4 us
    all_gather x1, waiting for transfers between devices, local(): lax.all_gather((tokens_normed * attn_norm).astype(jnp.bfloat16), 'mp', ax...  51.7 us
    all_gather x1, waiting for transfers between devices, local(): grad_full = lax.all_gather(grad_output, 'mp', axis=0, tiled=True)  49.6 us
    reduce_scatter x1, waiting for transfers between devices, local(): lax.psum_scatter(grad_pack.astype(jnp.bfloat16), 'ctx', scatter_dimension...  43.3 us
    psum x1, waiting for transfers between devices, together(): so_far = lax.psum(jnp.concatenate([a.ravel() for a in arrays]), axis)  42.1 us
  transfers between devices with their start and end apart: 10, of which 9 were waited for; matrix products, arithmetic and copies ran while one was open for 8% of the time, Pallas kernels for 0%

commit v1 on v0

v1 whole, which is shorter than its diff:
```python
import functools
import math

import jax
import jax.numpy as jnp
from jax import lax
from jax.experimental import pallas as pl
from jax.experimental.pallas import tpu as pltpu
from jax.sharding import PartitionSpec as P

EPSILON = 1e-05
ROPE_BASE = 1000000.0
MESH = pl.DeviceIdType.MESH
F32 = jnp.float32
BF16 = jnp.bfloat16
RELS = ("L", "R", "X", "O", "OL", "OR", "OX")
VMEM_LIMIT = 56 << 20


def params(cid):
    return pltpu.CompilerParams(
        collective_id=cid, has_side_effects=True, vmem_limit_bytes=VMEM_LIMIT
    )


def rel_index(axis, rel):
    me = lax.axis_index(axis)
    core = 0
    if axis == "ctx":
        core = lax.rem(me, 2)
        me = me // 2
    pos = lax.rem(me, 4)
    row = me // 4
    step = {"L": 3, "R": 1, "X": 2, "M": 0}[rel[-1] if rel[-1] != "O" else "M"]
    if rel[0] == "O":
        row = 1 - row
    index = row * 4 + lax.rem(pos + step, 4)
    if axis == "ctx":
        index = index * 2 + core
    return index


def sibling():
    me = lax.axis_index("ctx")
    return me + 1 - 2 * lax.rem(me, 2)


def enter(axes, sib=False, extra=()):
    barrier = pltpu.get_barrier_semaphore()
    count = 0
    for axis in axes:
        for rel in ("L", "R", "O"):
            pl.semaphore_signal(
                barrier, inc=1, device_id={axis: rel_index(axis, rel)}, device_id_type=MESH
            )
            count += 1
    if sib:
        pl.semaphore_signal(barrier, inc=1, device_id={"ctx": sibling()}, device_id_type=MESH)
        count += 1
    pl.semaphore_wait(barrier, count)


def rcopy(src, dst, ssem, rsem, axis, index):
    return pltpu.make_async_remote_copy(
        src_ref=src,
        dst_ref=dst,
        send_sem=ssem,
        recv_sem=rsem,
        device_id={axis: index},
        device_id_type=MESH,
    )


class Gather:
    scratch = (pltpu.SemaphoreType.DMA((28,)), pltpu.SemaphoreType.DMA((7, 4)))

    def __init__(self, axis, dst, ssem, rsem):
        self.axis, self.dst, self.ssem, self.rsem = axis, dst, ssem, rsem
        self.index = {rel: rel_index(axis, rel) for rel in RELS + ("M",)}
        self.sent = []
        self.seen = set()

    def send(self, source, p, to, as_rel):
        view = self.dst(self.index[source], p)
        copy = rcopy(
            view,
            view,
            self.ssem.at[len(self.sent)],
            self.rsem.at[RELS.index(as_rel), p],
            self.axis,
            self.index[to],
        )
        copy.start()
        self.sent.append(copy)

    def arrive(self, rel, p):
        if (rel, p) in self.seen:
            return
        self.seen.add((rel, p))
        view = self.dst(self.index[rel], p)
        rcopy(
            view, view, self.ssem.at[0], self.rsem.at[RELS.index(rel), p], self.axis, self.index["L"]
        ).wait_recv()

    def start_piece(self, p):
        if p < 2:
            self.send("M", p, "R", "L")
            self.send("M", p, "O", "O")
            self.send("M", p, "L", "R")
        else:
            self.send("M", p, "L", "R")
            self.send("M", p, "O", "O")
            self.send("M", p, "R", "L")

    def start(self):
        for p in (0, 2, 1, 3):
            self.start_piece(p)

    def relay_row(self):
        for a, b in ((0, 2), (1, 3)):
            self.arrive("L", a)
            self.send("L", a, "R", "X")
            self.arrive("R", b)
            self.send("R", b, "L", "X")

    def relay_opposite(self):
        for p in (0, 2, 1, 3):
            self.arrive("O", p)
            if p < 2:
                self.send("O", p, "R", "OL")
                self.send("O", p, "L", "OR")
            else:
                self.send("O", p, "L", "OR")
                self.send("O", p, "R", "OL")

    def relay_last(self):
        for a, b in ((0, 2), (1, 3)):
            self.arrive("OL", a)
            self.send("OL", a, "R", "OX")
            self.arrive("OR", b)
            self.send("OR", b, "L", "OX")

    def finish_piece(self, p):
        for rel in RELS:
            self.arrive(rel, p)

    def finish(self):
        for p in range(4):
            self.finish_piece(p)

    def drain(self):
        for copy in self.sent:
            copy.wait_send()

    def run(self):
        self.start()
        self.relay_row()
        self.relay_opposite()
        self.relay_last()
        self.finish()
        self.drain()


class Scatter:
    @staticmethod
    def scratch(piece):
        return (
            pltpu.VMEM((2, 2, 2) + piece, BF16),
            pltpu.VMEM((2, 2, 2) + piece, BF16),
            pltpu.VMEM((2, 2, 4) + piece, BF16),
            pltpu.VMEM((2, 4) + piece, BF16),
            pltpu.SemaphoreType.DMA((28,)),
            pltpu.SemaphoreType.DMA((28,)),
        )

    def __init__(self, axis, part, relay, stage, arrived, across, ssem, rsem):
        self.axis, self.part = axis, part
        self.relay, self.stage, self.arrived, self.across = relay, stage, arrived, across
        self.ssem, self.rsem = ssem, rsem
        self.index = {rel: rel_index(axis, rel) for rel in RELS + ("M",)}
        self.sent = []

    def block(self, t, rel, p):
        name = rel if t == 0 else ("O" if rel == "M" else "O" + rel)
        return self.part(self.index[name], p)

    def send(self, src, dst, rslot, to):
        copy = rcopy(
            src, dst, self.ssem.at[len(self.sent)], self.rsem.at[rslot], self.axis, self.index[to]
        )
        copy.start()
        self.sent.append(copy)

    def arrive(self, dst, rslot):
        rcopy(dst, dst, self.ssem.at[0], self.rsem.at[rslot], self.axis, self.index["L"]).wait_recv()

    def start(self, t):
        for q in range(2):
            self.send(self.block(t, "X", q), self.relay.at[0, t, q], t * 2 + q, "R")
            self.send(self.block(t, "X", 2 + q), self.relay.at[1, t, q], 4 + t * 2 + q, "L")
        for q in range(2):
            self.send(
                self.block(t, "R", 2 + q), self.arrived.at[0, t, 2 + q], 8 + t * 4 + 2 + q, "R"
            )
            self.send(self.block(t, "L", q), self.arrived.at[1, t, q], 16 + t * 4 + q, "L")

    def middle(self, t):
        for q in range(2):
            for d, to, p in ((0, "R", q), (1, "L", 2 + q)):
                self.arrive(self.relay.at[d, t, q], d * 4 + t * 2 + q)
                total = self.block(t, to, p)[...].astype(F32) + self.relay[d, t, q].astype(F32)
                self.stage[d, t, q] = total.astype(BF16)
                self.send(
                    self.stage.at[d, t, q], self.arrived.at[d, t, p], 8 + d * 8 + t * 4 + p, to
                )

    def row_sum(self, t, p):
        for d in range(2):
            self.arrive(self.arrived.at[d, t, p], 8 + d * 8 + t * 4 + p)
        return (
            self.block(t, "M", p)[...].astype(F32)
            + self.arrived[0, t, p].astype(F32)
            + self.arrived[1, t, p].astype(F32)
        )

    def cross(self):
        for p in (2, 0, 3, 1):
            self.across[0, p] = self.row_sum(1, p).astype(BF16)
            self.send(self.across.at[0, p], self.across.at[1, p], 24 + p, "O")

    def result(self, p):
        total = self.row_sum(0, p)
        self.arrive(self.across.at[1, p], 24 + p)
        return total + self.across[1, p].astype(F32)

    def begin(self):
        self.start(1)
        self.start(0)
        self.middle(1)
        self.cross()
        self.middle(0)

    def drain(self):
        for copy in self.sent:
            copy.wait_send()


def take(refs, count):
    return refs[:count], refs[count:]


def lane_iota(shape):
    return lax.broadcasted_iota(jnp.int32, shape, len(shape) - 1)


def dot_nt(a, b):
    return lax.dot_general(a, b, (((1,), (1,)), ((), ())), preferred_element_type=F32)


def dot_tn(a, b):
    return lax.dot_general(a, b, (((0,), (0,)), ((), ())), preferred_element_type=F32)


def dot(a, b):
    return jnp.dot(a, b, preferred_element_type=F32)


def head_sums(values, low):
    zero = jnp.zeros_like(values)
    first = jnp.sum(jnp.where(low, values, zero), axis=-1, keepdims=True)
    second = jnp.sum(jnp.where(low, zero, values), axis=-1, keepdims=True)
    return first, second


def swap_halves(values, first_half):
    return jnp.where(first_half, pltpu.roll(values, 96, 1), pltpu.roll(values, 32, 1))


def rms_scale(values):
    return lax.rsqrt(jnp.mean(values * values, axis=-1, keepdims=True) + EPSILON)


def norm_back(gradient, normed, scale_rows, gain_vec):
    scaled = gradient * gain_vec
    return scale_rows * (scaled - normed * jnp.mean(scaled * normed, axis=-1, keepdims=True))


def rows_of(index):
    return pl.ds(pl.multiple_of(index * 16, 16), 16)


def qkv_kernel(
    x, cot, gain1, w, gains, cosine, sine, full, cot_full, raw, queries, kv_all, *sems
):
    mp = lax.axis_index("mp")
    ctx = lax.axis_index("ctx")
    enter(("mp", "ctx"), sib=True)
    (s1, r1, s2, r2, s3, r3), (s4, r4) = take(sems, 6)
    for s in range(4):
        t = x[s].astype(F32)
        full[s, :, rows_of(mp), :] = (t * rms_scale(t) * gain1[...]).astype(BF16)
    first = Gather("mp", lambda i, p: full.at[p, :, rows_of(i), :], s1, r1)
    first.run()
    for s in range(4):
        cot_full[s, :, rows_of(mp), :] = cot[s]
    kv_view = lambda i, p: kv_all.at[p, pl.ds(i * 2, 2)]
    keys = Gather("ctx", kv_view, s2, r2)
    second = Gather("mp", lambda i, p: cot_full.at[p, :, rows_of(i), :], s3, r3)
    lane = lane_iota((256, 128))
    low = lane < 64
    first_half = lax.rem(lane, 64) < 32
    for s in range(4):
        y = dot(full[s].reshape(256, 1024), w[...])
        raw[s] = y
        a, b = y[:, :128], y[:, 128:]
        cos, sin = cosine[s], sine[s]
        lo, hi = head_sums(a * a, low)
        scale = jnp.where(
            low, lax.rsqrt(lo * (1 / 64) + EPSILON), lax.rsqrt(hi * (1 / 64) + EPSILON)
        )
        g = a * scale * gains[0:1, :]
        turned = g * cos + swap_halves(g, first_half) * sin
        zero = jnp.zeros_like(turned)
        head0 = jnp.where(low, turned, zero).astype(BF16)
        head1 = jnp.where(low, pltpu.roll(turned, 64, 1), zero).astype(BF16)
        for t in range(2):
            queries[s, t, 0:128] = head0[t * 128 : t * 128 + 128]
            queries[s, t, 128:256] = head1[t * 128 : t * 128 + 128]
        lo, _ = head_sums(b * b, low)
        g = b * lax.rsqrt(lo * (1 / 64) + EPSILON) * gains[1:2, :]
        turned = g * cos + swap_halves(g, first_half) * sin
        packed = jnp.where(low, turned, b).astype(BF16)
        kv_all[s, pl.ds(ctx * 2, 2)] = packed.reshape(2, 128, 128)
        keys.start_piece(s)
    second.start()
    sib = sibling()
    forwards = []

    def forward(rel, slot):
        view = kv_all.at[:, pl.ds(keys.index[rel] * 2, 2)]
        copy = rcopy(view, view, s4.at[slot], r4.at[slot], "ctx", sib)
        copy.start()
        forwards.append(copy)

    forward("M", 0)
    keys.relay_row()
    second.relay_row()
    keys.relay_opposite()
    second.relay_opposite()
    keys.relay_last()
    second.relay_last()
    for slot, rel in enumerate(RELS):
        for p in range(4):
            keys.arrive(rel, p)
        forward(rel, slot + 1)
    second.finish()
    keys.drain()
    second.drain()
    for copy in forwards:
        copy.wait_send()
    delta = sib - ctx
    for slot, rel in enumerate(("M",) + RELS):
        view = kv_all.at[:, pl.ds((keys.index[rel] + delta) * 2, 2)]
        rcopy(view, view, s4.at[slot], r4.at[slot], "ctx", sib).wait_recv()


def attention_kernel(own, where, queries, kv_all, low_out, high_out, logs, acc):
    lane_k = lane_iota((256, 128)) < 64
    for j in range(2):
        mine = own[j]
        acc[...] = jnp.zeros_like(acc)

        def step(i, masked):
            slot0, slot1 = where[2 * i], where[2 * i + 1]
            if masked:
                row = lax.rem(lax.broadcasted_iota(jnp.int32, (256, 256), 0), 128)
                col = lax.broadcasted_iota(jnp.int32, (256, 256), 1)
                keep = col + 256 * i <= row + 128 * mine
            for s in range(4):
                kv = jnp.concatenate([kv_all[s, slot0], kv_all[s, slot1]], axis=0)
                weights = jnp.exp(dot_nt(queries[s, j], kv) * 0.125)
                if masked:
                    weights = jnp.where(keep, weights, 0.0)
                ones = jnp.where(lane_k, jnp.ones_like(kv), kv)
                acc[s] += dot(weights.astype(BF16), ones)

        last = mine // 2
        lax.fori_loop(0, last, lambda i, c: (step(i, False), c)[1], 0)
        step(last, True)
        low = lane_iota((128, 128)) < 64
        for s in range(4):
            a = acc[s]
            o = a * pltpu.roll(1.0 / a, 64, 1)
            both = jnp.where(low, pltpu.roll(o[0:128], 64, 1), o[128:256])
            low_out[s, j] = both.astype(BF16)
            high_out[s, j] = both
            logs[s, j] = jnp.log(a.T[0:8])


def attention_back_kernel(
    own, where, queries, kv_all, grad_out, out, logs, grad_q, grad_kv, acc, grad_pad, turned, delta
):
    acc[...] = jnp.zeros_like(acc)
    low = lane_iota((128, 128)) < 64
    for j in range(2):
        mine = own[j]
        turned[...] = jnp.zeros_like(turned)
        for s in range(4):
            g = grad_out[s, j]
            gf = g.astype(F32)
            zero = jnp.zeros_like(gf)
            grad_pad[s, 0:128] = jnp.where(low, zero, pltpu.roll(gf, 64, 1)).astype(BF16)
            grad_pad[s, 128:256] = jnp.where(low, zero, gf).astype(BF16)
            product = (gf * out[s, j]).T
            delta[s, :, 0:128] = jnp.broadcast_to(
                jnp.sum(product[0:64], axis=0, keepdims=True), (8, 128)
            )
            delta[s, :, 128:256] = jnp.broadcast_to(
                jnp.sum(product[64:128], axis=0, keepdims=True), (8, 128)
            )

        def step(i, masked):
            slot0, slot1 = where[2 * i], where[2 * i + 1]
            if masked:
                col = lax.rem(lax.broadcasted_iota(jnp.int32, (256, 256), 1), 128)
                row = lax.broadcasted_iota(jnp.int32, (256, 256), 0)
                keep = row + 256 * i <= col + 128 * mine
            for s in range(4):
                kv = jnp.concatenate([kv_all[s, slot0], kv_all[s, slot1]], axis=0)
                q, g = queries[s, j], grad_pad[s]
                probs = jnp.exp(dot_nt(kv, q) * 0.125 - logs[s, j, 0:1])
                if masked:
                    probs = jnp.where(keep, probs, 0.0)
                scores = (probs * (dot_nt(kv, g) - delta[s, 0:1])).astype(BF16)
                turned[s] += dot_tn(kv, scores)
                block = dot(
                    jnp.concatenate([scores, probs.astype(BF16)], axis=1),
                    jnp.concatenate([q, g], axis=0),
                )
                acc[s, slot0] += block[0:128]
                acc[s, slot1] += block[128:256]

        last = mine // 2
        lax.fori_loop(0, last, lambda i, c: (step(i, False), c)[1], 0)
        step(last, True)
        for s in range(4):
            t = turned[s].T * 0.125
            grad_q[s, j] = jnp.where(low, t[0:128], pltpu.roll(t[128:256], 64, 1))
    scale = jnp.where(low, 0.125, 1.0)

    def finish(n, c):
        for s in range(4):
            grad_kv[s, n] = (acc[s, n] * scale).astype(BF16)
        return c

    lax.fori_loop(0, 32, finish, 0)


def mix_kernel(x, attended, w, gain2, mixed, full, part, *scratch):
    mp = lax.axis_index("mp")
    enter(("mp",))
    sums, (s1, r1) = take(scratch, 6)
    for s in range(4):
        rows = dot(attended[s].reshape(256, 128), w[...])
        part[s] = rows.astype(BF16).reshape(2, 128, 1024)
    scatter = Scatter("mp", lambda i, p: part.at[p, :, rows_of(i), :], *sums)
    scatter.begin()
    gather = Gather("mp", lambda i, p: full.at[p, :, rows_of(i), :], s1, r1)
    for p in (2, 0, 3, 1):
        m = x[p].astype(F32) + scatter.result(p)
        mixed[p] = m
        full[p, :, rows_of(mp), :] = (m * rms_scale(m) * gain2[...]).astype(BF16)
        gather.start_piece(p)
    gather.relay_row()
    gather.relay_opposite()
    gather.relay_last()
    gather.finish()
    scatter.drain()
    gather.drain()


def branch_kernel(
    part_d, part_o, mixed, cot, gain2, w, out, d_mixed, full, d_att, gain_part, *scratch
):
    mp = lax.axis_index("mp")
    enter(("mp",))
    sums_d, rest = take(scratch, 6)
    sums_o, (s1, r1) = take(rest, 6)
    scatter = Scatter("mp", lambda i, p: part_d.at[p, :, rows_of(i), :], *sums_d)
    scatter.begin()
    other = Scatter("mp", lambda i, p: part_o.at[p, :, rows_of(i), :], *sums_o)
    gather = Gather("mp", lambda i, p: full.at[p, :, rows_of(i), :], s1, r1)
    gain_sum = jnp.zeros((1, 1024), F32)
    for p in (2, 0, 3, 1):
        g = scatter.result(p)
        m = mixed[p]
        scale = rms_scale(m)
        normed = m * scale
        gain_sum += jnp.sum((g * normed).reshape(32, 1024), axis=0, keepdims=True)
        dm = cot[p].astype(F32) + norm_back(g, normed, scale, gain2[...])
        d_mixed[p] = dm
        full[p, :, rows_of(mp), :] = dm.astype(BF16)
        gather.start_piece(p)
    gain_part[...] = gain_sum
    gather.relay_row()
    gather.relay_opposite()
    gather.relay_last()
    other.start(1)
    other.start(0)
    gather.finish()
    for s in range(4):
        d_att[s] = dot_nt(full[s].reshape(256, 1024), w[...]).astype(BF16).reshape(2, 128, 128)
    other.middle(1)
    other.cross()
    other.middle(0)
    for p in (2, 0, 3, 1):
        out[p] = (mixed[p] + other.result(p)).astype(BF16)
    scatter.drain()
    gather.drain()
    other.drain()


def last_kernel(
    grad_kv, grad_q, raw, cosine, sine, gains, w, x, gain1, d_mixed,
    d_qkv, in_grad, gain_part, head_part,
    pair, arrived, part, *scratch,
):
    ctx = lax.axis_index("ctx")
    enter(("mp", "ctx"), sib=True)
    sums_k, rest = take(scratch, 6)
    sums_n, (s1, r1) = take(rest, 6)
    core = lax.rem(ctx, 2)
    sib = sibling()
    copies = []
    for chip in range(8):
        src = grad_kv.at[:, pl.ds(chip * 4 + (1 - core) * 2, 2)]
        copy = rcopy(src, arrived.at[:, pl.ds(chip * 2, 2)], s1.at[chip], r1.at[chip], "ctx", sib)
        copy.start()
        copies.append(copy)
    for chip in range(8):
        copies[chip].wait_recv()
        for s in range(4):
            mine = grad_kv[s, pl.ds(chip * 4 + core * 2, 2)].astype(F32)
            pair[s, chip * 2 : chip * 2 + 2] = (
                mine + arrived[s, chip * 2 : chip * 2 + 2].astype(F32)
            ).astype(BF16)
    scatter = Scatter("ctx", lambda i, p: pair.at[p, pl.ds((i // 2) * 2, 2)], *sums_k)
    scatter.begin()
    lane = lane_iota((256, 128))
    low = lane < 64
    first_half = lax.rem(lane, 64) < 32
    inv = 1 / 64
    head_q = jnp.zeros((1, 128), F32)
    head_k = jnp.zeros((1, 128), F32)
    for s in (2, 0, 3, 1):
        y = raw[s]
        a, b = y[:, :128], y[:, 128:]
        cos, sin = cosine[s], sine[s]
        lo, hi = head_sums(a * a, low)
        scale = jnp.where(low, lax.rsqrt(lo * inv + EPSILON), lax.rsqrt(hi * inv + EPSILON))
        n = a * scale
        d = grad_q[s].reshape(256, 128)
        g = d * cos - swap_halves(d, first_half) * sin
        head_q += jnp.sum(g * n, axis=0, keepdims=True)
        e = g * gains[0:1, :]
        lo, hi = head_sums(e * n, low)
        dq = scale * (e - n * jnp.where(low, lo * inv, hi * inv))
        d_qkv[s, :, 0:128] = dq.astype(BF16)
        lo, _ = head_sums(b * b, low)
        scale = lax.rsqrt(lo * inv + EPSILON)
        n = b * scale
        d = scatter.result(s).reshape(256, 128)
        g = d * cos - swap_halves(d, first_half) * sin
        head_k += jnp.sum(g * n, axis=0, keepdims=True)
        e = g * gains[1:2, :]
        lo, _ = head_sums(e * n, low)
        dk = scale * (e - n * (lo * inv))
        d_qkv[s, :, 128:256] = jnp.where(low, dk, d).astype(BF16)
        part[s] = dot_nt(d_qkv[s], w[...]).astype(BF16).reshape(2, 128, 1024)
    head_part[0:1, :] = head_q
    head_part[1:2, :] = head_k
    total = Scatter("mp", lambda i, p: part.at[p, :, rows_of(i), :], *sums_n)
    total.begin()
    gain_sum = jnp.zeros((1, 1024), F32)
    for p in (2, 0, 3, 1):
        g = total.result(p)
        t = x[p].astype(F32)
        scale = rms_scale(t)
        normed = t * scale
        gain_sum += jnp.sum((g * normed).reshape(32, 1024), axis=0, keepdims=True)
        in_grad[p] = (d_mixed[p] + norm_back(g, normed, scale, gain1[...])).astype(BF16)
    gain_part[...] = gain_sum
    for copy in copies:
        copy.wait_send()
    scatter.drain()
    total.drain()


def reduce_kernel(ffn, attn, ffn_out, attn_out, pair_f, pair_a, got_f, got_a, *scratch):
    enter(("ctx",), sib=True)
    sums_f, rest = take(scratch, 6)
    sums_a, rest = take(rest, 6)
    (sf, rf, sa, ra), (s1, r1) = take(rest, 4)
    ctx = lax.axis_index("ctx")
    core = lax.rem(ctx, 2)
    sib = sibling()

    def rows64(i):
        return pl.ds(pl.multiple_of(i * 64, 64), 64)

    copies = []
    for chip in range(8):
        for n, (src, got) in enumerate(((ffn, got_f), (attn, got_a))):
            copy = rcopy(
                src.at[:, rows64(chip * 2 + 1 - core), :],
                got.at[:, rows64(chip), :],
                s1.at[n, chip],
                r1.at[n, chip],
                "ctx",
                sib,
            )
            copy.start()
            copies.append(copy)
    work = ((ffn, got_f, pair_f), (attn, got_a, pair_a))
    for chip in range(8):
        for n, (src, got, pair) in enumerate(work):
            copies[chip * 2 + n].wait_recv()
            rows = slice(chip * 64, chip * 64 + 64)
            mine = src[:, rows64(chip * 2 + core), :].astype(F32)
            pair[:, rows, :] = (mine + got[:, rows, :].astype(F32)).astype(BF16)

    def piece(ref, i, p):
        return ref.at[:, pl.ds(pl.multiple_of((i // 2) * 64 + p * 16, 16), 16), :]

    def place(ref, i, p):
        return ref.at[:, pl.ds(pl.multiple_of(i * 64 + p * 16, 16), 16), :]

    scat_f = Scatter("ctx", lambda i, p: piece(pair_f, i, p), *sums_f)
    scat_a = Scatter("ctx", lambda i, p: piece(pair_a, i, p), *sums_a)
    scat_f.begin()
    scat_a.begin()
    gath_f = Gather("ctx", lambda i, p: place(ffn_out, i, p), sf, rf)
    gath_a = Gather("ctx", lambda i, p: place(attn_out, i, p), sa, ra)
    for p in (2, 0, 3, 1):
        place(ffn_out, ctx, p)[...] = scat_f.result(p).astype(BF16)
        gath_f.start_piece(p)
    for p in (2, 0, 3, 1):
        place(attn_out, ctx, p)[...] = scat_a.result(p).astype(BF16)
        gath_a.start_piece(p)
    forwards = []

    def forward(ref, n, index, slot):
        view = ref.at[:, rows64(index), :]
        copy = rcopy(view, view, s1.at[2 + n, slot], r1.at[2 + n, slot], "ctx", sib)
        copy.start()
        forwards.append(copy)

    forward(ffn_out, 0, ctx, 0)
    forward(attn_out, 1, ctx, 0)
    for phase in ("relay_row", "relay_opposite", "relay_last"):
        getattr(gath_f, phase)()
        getattr(gath_a, phase)()
    for slot, rel in enumerate(RELS):
        for n, (gath, ref) in enumerate(((gath_f, ffn_out), (gath_a, attn_out))):
            for p in range(4):
                gath.arrive(rel, p)
            forward(ref, n, gath.index[rel], slot + 1)
    for copy in copies + forwards:
        copy.wait_send()
    for slot, rel in enumerate(("M",) + RELS):
        for n, ref in enumerate((ffn_out, attn_out)):
            view = ref.at[:, rows64(gath_f.index[rel] + sib - ctx), :]
            rcopy(view, view, s1.at[2 + n, slot], r1.at[2 + n, slot], "ctx", sib).wait_recv()
    for item in (scat_f, scat_a, gath_f, gath_a):
        item.drain()


def gains_kernel(parts, total, by_mp, by_ctx, s1, r1, s2, r2):
    mp, ctx = lax.axis_index("mp"), lax.axis_index("ctx")
    barrier = pltpu.get_barrier_semaphore()
    for k in range(1, 8):
        pl.semaphore_signal(
            barrier, inc=1, device_id={"mp": lax.rem(mp + k, 8)}, device_id_type=MESH
        )
    for k in range(1, 16):
        pl.semaphore_signal(
            barrier, inc=1, device_id={"ctx": lax.rem(ctx + k, 16)}, device_id_type=MESH
        )
    pl.semaphore_wait(barrier, 22)
    copies = []
    for k in range(1, 8):
        copy = rcopy(
            parts, by_mp.at[k], s1.at[k], r1.at[k], "mp", lax.rem(mp + k, 8)
        )
        copy.start()
        copies.append(copy)
    by_mp[0] = parts[...]
    for copy in copies:
        copy.wait()
    mine = jnp.sum(by_mp[...], axis=0)
    by_ctx[0] = mine
    copies = []
    for k in range(1, 16):
        copy = rcopy(
            by_ctx.at[0], by_ctx.at[k], s2.at[k], r2.at[k], "ctx", lax.rem(ctx + k, 16)
        )
        copy.start()
        copies.append(copy)
    for copy in copies:
        copy.wait()
    total[...] = jnp.zeros_like(total)

    def add(i, c):
        total[...] += by_ctx[lax.rem(ctx - i + 16, 16)]
        return c

    lax.fori_loop(0, 16, add, 0)


def vm(n):
    return [pl.BlockSpec(memory_space=pltpu.VMEM)] * n


def sds(shape, dtype):
    return jax.ShapeDtypeStruct(shape, dtype)


def local(
    residual_in,
    attn_norm,
    query_key_value_weight,
    query_gain,
    key_gain,
    out_weight,
    ffn_norm,
    gate_up,
    down_weight,
    cotangent,
    positions,
    block_map,
):
    ctx_index = lax.axis_index("ctx")
    rows_shape = (4, 2, 16, 1024)
    full_shape = (4, 2, 128, 1024)
    piece = (2, 16, 1024)
    kv_piece = (2, 128, 128)
    dma = pltpu.SemaphoreType.DMA

    own = lax.dynamic_slice_in_dim(block_map, ctx_index * 2, 2)
    where = jnp.sum(
        jnp.where(block_map[None, :] == jnp.arange(32)[:, None], jnp.arange(32)[None, :], 0),
        axis=1,
    ).astype(jnp.int32)
    position = jnp.concatenate(
        [lax.dynamic_slice_in_dim(positions, own[j] * 128, 128, 1) for j in range(2)], axis=1
    ).astype(F32)
    inverse_freq = 1.0 / ROPE_BASE ** (jnp.arange(0, 64, 2, dtype=F32) / 64)
    angles = position[:, :, None] * inverse_freq
    cos32, sin32 = jnp.cos(angles), jnp.sin(angles)
    cosine = jnp.concatenate([cos32] * 4, axis=-1)
    sine = jnp.concatenate([-sin32, sin32] * 2, axis=-1)
    gains = jnp.stack(
        [jnp.concatenate([query_gain] * 2), jnp.concatenate([key_gain, jnp.ones_like(key_gain)])]
    )
    gain1 = attn_norm.reshape(1, 1024)
    gain2 = ffn_norm.reshape(1, 1024)
    w_qkv = query_key_value_weight.reshape(1024, 256)

    full1, cot_full, raw, queries, kv_all = pl.pallas_call(
        qkv_kernel,
        out_shape=(
            sds(full_shape, BF16),
            sds(full_shape, BF16),
            sds((4, 256, 256), F32),
            sds((4, 2, 256, 128), BF16),
            sds((4, 32, 128, 128), BF16),
        ),
        in_specs=vm(7),
        out_specs=tuple(vm(5)),
        scratch_shapes=Gather.scratch * 3 + (dma((8,)), dma((8,))),
        compiler_params=params(1),
    )(residual_in, cotangent, gain1, w_qkv, gains, cosine, sine)

    smem = [pl.BlockSpec(memory_space=pltpu.SMEM)] * 2
    attended, attended_high, logs = pl.pallas_call(
        attention_kernel,
        out_shape=(
            sds((4, 2, 128, 128), BF16),
            sds((4, 2, 128, 128), F32),
            sds((4, 2, 8, 256), F32),
        ),
        in_specs=smem + vm(2),
        out_specs=tuple(vm(3)),
        scratch_shapes=[pltpu.VMEM((4, 256, 128), F32)],
        compiler_params=pltpu.CompilerParams(vmem_limit_bytes=VMEM_LIMIT),
    )(own, where, queries, kv_all)

    mixed, full2 = pl.pallas_call(
        mix_kernel,
        out_shape=(sds(rows_shape, F32), sds(full_shape, BF16)),
        in_specs=vm(4),
        out_specs=tuple(vm(2)),
        scratch_shapes=(pltpu.VMEM(full_shape, BF16),) + Scatter.scratch(piece) + Gather.scratch,
        compiler_params=params(2),
    )(residual_in, attended, out_weight, gain2)

    rows2 = full2.reshape(1024, 1024)
    cot_rows = cot_full.reshape(1024, 1024)
    gate = dot(rows2, gate_up[:, 0, :])
    up = dot(rows2, gate_up[:, 1, :])
    sig = jax.nn.sigmoid(gate)
    active = (gate * sig * up).astype(BF16)
    part_o = dot(active, down_weight).astype(BF16)
    d_active = dot_nt(cot_rows, down_weight)
    d_gate = (d_active * up * sig * (1.0 + gate * (1.0 - sig))).astype(BF16)
    d_up = (d_active * gate * sig).astype(BF16)
    part_d = (dot_nt(d_gate, gate_up[:, 0, :]) + dot_nt(d_up, gate_up[:, 1, :])).astype(BF16)
    ffn_grads = jnp.stack(
        [
            dot_tn(rows2, d_gate).astype(BF16),
            dot_tn(rows2, d_up).astype(BF16),
            dot_tn(cot_rows, active).astype(BF16),
        ]
    )

    output, d_mixed, branch, d_att, gain2_part = pl.pallas_call(
        branch_kernel,
        out_shape=(
            sds(rows_shape, BF16),
            sds(rows_shape, F32),
            sds(full_shape, BF16),
            sds((4, 2, 128, 128), BF16),
            sds((1, 1024), F32),
        ),
        in_specs=vm(6),
        out_specs=tuple(vm(5)),
        scratch_shapes=Scatter.scratch(piece) * 2 + Gather.scratch,
        compiler_params=params(3),
    )(part_d.reshape(full_shape), part_o.reshape(full_shape), mixed, cotangent, gain2, out_weight)

    grad_q, grad_kv = pl.pallas_call(
        attention_back_kernel,
        out_shape=(sds((4, 2, 128, 128), F32), sds((4, 32, 128, 128), BF16)),
        in_specs=smem + vm(5),
        out_specs=tuple(vm(2)),
        scratch_shapes=[
            pltpu.VMEM((4, 32, 128, 128), F32),
            pltpu.VMEM((4, 256, 128), BF16),
            pltpu.VMEM((4, 128, 256), F32),
            pltpu.VMEM((4, 8, 256), F32),
        ],
        compiler_params=pltpu.CompilerParams(vmem_limit_bytes=VMEM_LIMIT),
    )(own, where, queries, kv_all, d_att, attended_high, logs)

    d_qkv, input_grad, gain1_part, head_part = pl.pallas_call(
        last_kernel,
        out_shape=(
            sds((4, 256, 256), BF16),
            sds(rows_shape, BF16),
            sds((1, 1024), F32),
            sds((2, 128), F32),
        ),
        in_specs=vm(10),
        out_specs=tuple(vm(4)),
        scratch_shapes=(
            pltpu.VMEM((4, 16, 128, 128), BF16),
            pltpu.VMEM((4, 16, 128, 128), BF16),
            pltpu.VMEM(full_shape, BF16),
        )
        + Scatter.scratch(kv_piece)
        + Scatter.scratch(piece)
        + (dma((8,)), dma((8,))),
        compiler_params=params(4),
    )(
        grad_kv, grad_q, raw, cosine, sine, gains, w_qkv, residual_in, gain1, d_mixed
    )

    qkv_part = dot_tn(full1.reshape(1024, 1024), d_qkv.reshape(1024, 256))
    out_part = dot_tn(branch.reshape(1024, 1024), attended.reshape(1024, 128))
    attn_grads = jnp.concatenate([qkv_part.astype(BF16), out_part.astype(BF16)], axis=1)[None]
    ffn_sum, attn_sum = pl.pallas_call(
        reduce_kernel,
        out_shape=(sds((3, 1024, 576), BF16), sds((1, 1024, 384), BF16)),
        in_specs=vm(2),
        out_specs=tuple(vm(2)),
        scratch_shapes=(
            pltpu.VMEM((3, 512, 576), BF16),
            pltpu.VMEM((1, 512, 384), BF16),
            pltpu.VMEM((3, 512, 576), BF16),
            pltpu.VMEM((1, 512, 384), BF16),
        )
        + Scatter.scratch((3, 16, 576))
        + Scatter.scratch((1, 16, 384))
        + Gather.scratch * 2
        + (dma((4, 8)), dma((4, 8))),
        compiler_params=params(5),
    )(ffn_grads, attn_grads)

    head_sum = head_part[0, :64] + head_part[0, 64:]
    small = jnp.concatenate(
        [
            gain1_part,
            gain2_part,
            jnp.pad(jnp.concatenate([head_sum, head_part[1, :64]]), (0, 896))[None],
            jnp.zeros((5, 1024), F32),
        ]
    )
    sums = pl.pallas_call(
        gains_kernel,
        out_shape=sds((8, 1024), F32),
        in_specs=vm(1),
        out_specs=vm(1)[0],
        scratch_shapes=[
            pltpu.VMEM((8, 8, 1024), F32),
            pltpu.VMEM((16, 8, 1024), F32),
            dma((8,)),
            dma((8,)),
            dma((16,)),
            dma((16,)),
        ],
        compiler_params=params(6),
    )(small)

    return (
        output,
        input_grad,
        sums[0],
        attn_sum[0, :, :256].astype(F32).reshape(1024, 1, 256),
        sums[2, :64],
        sums[2, 64:128],
        attn_sum[0, :, 256:].astype(F32).T,
        sums[1],
        jnp.stack([ffn_sum[0], ffn_sum[1]], axis=1).astype(F32),
        ffn_sum[2].astype(F32).T,
    )


def solution(mesh):
    return jax.shard_map(
        local,
        mesh=mesh,
        in_specs=(
            P(None, "ctx", "mp", None),
            P(),
            P(None, "mp", None),
            P(),
            P(),
            P("mp", None),
            P(),
            P(None, None, "mp"),
            P("mp", None),
            P(None, "ctx", "mp", None),
            P(),
            P(),
        ),
        out_specs=(
            P(None, "ctx", "mp", None),
            P(None, "ctx", "mp", None),
            P(),
            P(None, "mp", None),
            P(),
            P(),
            P("mp", None),
            P(),
            P(None, None, "mp"),
            P("mp", None),
        ),
        check_vma=False,
    )
```

time: 915 us -> 419 us (0.46)
  waiting for transfers between devices: 418 us -> 0 us
  Pallas kernels: 0 us -> 345 us
  local copies, waits for them, and re-layouts: 119 us -> 18.4 us
  blocking collectives: 98.8 us -> 0 us
  matrix products: 122 us -> 25.5 us
  other arithmetic: 84.1 us -> 20.4 us
  loops' own time: 33.1 us -> 0 us
  starting transfers between devices: 14.9 us -> 0 us
  between operations: 14.9 us -> 2.37 us
    pallas_call x0 -> x8, Pallas kernels: none -> 345 us  [the longest x1 63.5 us: local(): pl.pallas_call(branch_kernel, out_shape=(sds(rows_shape, BF16), sds(rows_...]
    all_gather x5 -> x0, waiting for transfers between devices: 232 us -> none  [the longest x1 53 us: local(): lax.all_gather((mixed_normed * ffn_norm).astype(jnp.bfloat16), 'mp', axis...]
    reduce_scatter x2 -> x0, waiting for transfers between devices: 119 us -> none  [the longest x1 75.4 us: local(): lax.psum_scatter(jnp.dot(attended_rows, out_weight, preferred_element_typ...]
    dot_general x68 -> x11, matrix products: 122 us -> 25.5 us  [the longest x5 9.74 us: dot_tn(): lax.dot_general(a, b, (((0,), (0,)), ((), ())), preferred_element_type=F32)]
    psum x1 -> x0, blocking collectives: 68.8 us -> none  [local(): lax.psum((attn_norm_part, ffn_norm_part, query_gain_part, key_gain_part),...]
    psum x1 -> x0, waiting for transfers between devices: 42.1 us -> none  [together(): so_far = lax.psum(jnp.concatenate([a.ravel() for a in arrays]), axis)]
    dynamic_slice x24 -> x2, local copies, waits for them, and re-layouts: 36.1 us -> 1.53 us  [the longest x1 0.83 us: local(): own = lax.dynamic_slice_in_dim(block_map, ctx_index * 2, 2)]
    another operation x27 -> x0, loops' own time: 33.1 us -> none  [the longest x1 10.6 us: local(): lax.fori_loop(0, group_count, stats_step, (jnp.full(row_shape, -1e+30, jn...]
  transfers between devices with their start and end apart: 10 -> 0, of which waited for: 9 -> 0; matrix products, arithmetic and copies ran while one was open for 8% -> 0% of each run, Pallas kernels for 0% -> 0%
where the time goes in v1:
time: 419 us; the launch traced here: 412 us
  Pallas kernels  345 us (82%)
  matrix products  25.5 us (6%)
  other arithmetic  20.4 us (5%)
  local copies, waits for them, and re-layouts  18.4 us (4%)
    pallas_call x1, Pallas kernels, local(): pl.pallas_call(branch_kernel, out_shape=(sds(rows_shape, BF16), sds(rows_...  63.5 us
    pallas_call x1, Pallas kernels, local(): pl.pallas_call(reduce_kernel, out_shape=(sds((3, 1024, 576), BF16), sds((...  60.3 us
    pallas_call x1, Pallas kernels, local(): pl.pallas_call(last_kernel, out_shape=(sds((4, 256, 256), BF16), sds(rows...  56.9 us
    pallas_call x1, Pallas kernels, local(): pl.pallas_call(qkv_kernel, out_shape=(sds(full_shape, BF16), sds(full_sha...  55.2 us
    pallas_call x1, Pallas kernels, local(): pl.pallas_call(mix_kernel, out_shape=(sds(rows_shape, F32), sds(full_shap...  46.2 us
    pallas_call x1, Pallas kernels, local(): pl.pallas_call(attention_back_kernel, out_shape=(sds((4, 2, 128, 128), F3...  28.9 us
    pallas_call x1, Pallas kernels, local(): pl.pallas_call(gains_kernel, out_shape=sds((8, 1024), F32), in_specs=vm(1...  18.2 us
    pallas_call x1, Pallas kernels, local(): pl.pallas_call(attention_kernel, out_shape=(sds((4, 2, 128, 128), BF16),...  15.6 us

profile of v1, /device:TPU:0, one launch (start us, length us, event | category | flops | bytes accessed | tf_op | source)
XLA Modules:
  0.0 411.5 jit_solution(13316826514024644391)
XLA Ops:
  6.8 1.9 fusion.15
  10.6 55.2 %shard_map.195 = (bf16[4,2,128,1024]{3,2,1,0:T(8,128)(2,1)}, bf16[4,2,128,1024]{3,2,1,0:T(8,128)(2,1)}, f32[4,256,256]{2,1,0:T(8,128)}, bf16[4,2,256,128]{3,2,1,0:T(8,128)(2,1)}, bf16[4,32,128,128]{3,2,1,0:T(8,128)(2,1)}) custom-call(bf16[4,2,16,1024]{3,2,1,0:T(8,128)(2,1)} %x.9, bf16[4,2,16,1024]{3,2,1,0:T(8,128)(2,1)} %cot.3, f32[1,1024]{1,0:T(1,128)} %bitcast.89, ...), custom_call_target="tpu_custom_call" | custom-call | tf_op jit(solution)/shard_map/pallas_call | solution.py:769
  65.8 15.6 %shard_map.196 = (bf16[4,2,128,128]{3,2,1,0:T(8,128)(2,1)}, f32[4,2,128,128]{3,2,1,0:T(8,128)}, f32[4,2,8,256]{3,2,1,0:T(8,128)}) custom-call(s32[2]{0:T(128)} %copy-done.6, s32[32]{0:T(128)} %select_reduce_fusion.where, bf16[4,2,256,128]{3,2,1,0:T(8,128)(2,1)} %get-tuple-element.34.queries, bf16[4,32,128,128]{3,2,1,0:T(8,128)(2,1)} %get-tuple-element.35.kv_all), custom_call_target="tpu_custom_call" | custom-call | tf_op jit(solution)/shard_map/pallas_call | solution.py:785
  82.9 46.2 %shard_map.197 = (f32[4,2,16,1024]{3,2,1,0:T(8,128)}, bf16[4,2,128,1024]{3,2,1,0:T(8,128)(2,1)}) custom-call(bf16[4,2,16,1024]{3,2,1,0:T(8,128)(2,1)} %x.9, bf16[4,2,128,128]{3,2,1,0:T(8,128)(2,1)} %get-tuple-element.36.attended, bf16[128,1024]{1,0:T(8,128)(2,1)} %w.3, f32[1,1024]{1,0:T(1,128)} %bitcast.92), custom_call_target="tpu_custom_call" | custom-call | tf_op jit(solution)/shard_map/pallas_call | solution.py:798
  129.1 3.2 fusion.6
  132.3 2.8 multiply_convert_fusion
  135.1 1.9 fusion.2
  137.0 3.2 convolution_convert_fusion
  140.1 1.9 fusion
  142.0 1.9 fusion.1
  143.9 2.7 pad_maximum_fusion.ffn
  146.6 1.9 fusion.4
  148.4 3.3 add_convert_fusion
  151.7 63.5 %shard_map.198 = (bf16[4,2,16,1024]{3,2,1,0:T(8,128)(2,1)}, f32[4,2,16,1024]{3,2,1,0:T(8,128)}, bf16[4,2,128,1024]{3,2,1,0:T(8,128)(2,1)}, bf16[4,2,128,128]{3,2,1,0:T(8,128)(2,1)}, f32[1,1024]{1,0:T(1,128)}) custom-call(bf16[4,2,128,1024]{3,2,1,0:T(8,128)(2,1)} %bitcast.86, bf16[4,2,128,1024]{3,2,1,0:T(8,128)(2,1)} %bitcast.85, ...), custom_call_target="tpu_custom_call" | custom-call | tf_op jit(solution)/shard_map/pallas_call | solution.py:826
  215.3 2.4 fusion.3
  217.6 28.9 %shard_map.199 = (f32[4,2,128,128]{3,2,1,0:T(8,128)}, bf16[4,32,128,128]{3,2,1,0:T(8,128)(2,1)}) custom-call(s32[2]{0:T(128)} %copy-done.6, s32[32]{0:T(128)} %select_reduce_fusion.where, bf16[4,2,256,128]{3,2,1,0:T(8,128)(2,1)} %get-tuple-element.34.queries, bf16[4,32,128,128]{3,2,1,0:T(8,128)(2,1)} %get-tuple-element.35.kv_all, ...), custom_call_target="tpu_custom_call" | custom-call | tf_op jit(solution)/shard_map/pallas_call | solution.py:841
  246.6 56.9 %shard_map.200 = (bf16[4,256,256]{2,1,0:T(8,128)(2,1)}, bf16[4,2,16,1024]{3,2,1,0:T(8,128)(2,1)}, f32[1,1024]{1,0:T(1,128)}, f32[2,128]{1,0:T(2,128)}) custom-call(bf16[4,32,128,128]{3,2,1,0:T(8,128)(2,1)} %get-tuple-element.43.grad_kv, f32[4,2,128,128]{3,2,1,0:T(8,128)} %get-tuple-element.44.grad_q, f32[4,256,256]{2,1,0:T(8,128)} %get-tuple-element.45.raw, ...), custom_call_target="tpu_custom_call" | custom-call | tf_op jit(solution)/shard_map/pallas_call | solution.py:855
  306.2 60.3 %shard_map.202 = (bf16[3,1024,576]{2,1,0:T(8,128)(2,1)}, bf16[1,1024,384]{2,1,0:T(8,128)(2,1)}) custom-call(bf16[3,1024,576]{2,1,0:T(8,128)(2,1)} %pad_maximum_fusion.ffn, bf16[1,1024,384]{2,1,0:T(8,128)(2,1)} %maximum_bitcast_fusion.attn), custom_call_target="tpu_custom_call" | custom-call | tf_op jit(solution)/shard_map/pallas_call | solution.py:881
  367.4 18.2 %shard_map.201 = f32[8,1024]{1,0:T(8,128)} custom-call(f32[8,1024]{1,0:T(8,128)} %maximum_maximum_fusion.parts), custom_call_target="tpu_custom_call" | custom-call | tf_op jit(solution)/shard_map/pallas_call | solution.py:908
  390.5 2.0 copy.38
  392.5 4.4 %convert_bitcast_fusion = (f32[576,1024]{0,1:T(8,128)}, bf16[1024,1,576]{2,0,1:T(8,128)(2,1)S(1)}, bf16[1024,1,576]{2,0,1:T(8,128)(2,1)}) fusion(bf16[3,1024,576]{2,1,0:T(8,128)(2,1)} %get-tuple-element.55), kind=kLoop, calls=%fused_computation.3 | loop fusion | flops 589824 | bytes 8257536 | tf_op jit(solution)/shard_map/transpose | solution.py:934
  396.9 3.1 copy.41
  400.0 4.1 maximum_convert_fusion
  404.1 5.8 %copy.40 = f32[1024,2,576]{0,2,1:T(8,128)} copy(f32[1024,2,576]{2,0,1:T(8,128)} %maximum_convert_fusion) | data formatting | bytes 9437184
  (52 shorter events, 18.0 us)
Async XLA Ops:
  0.6 80.8 %copy-start = (bf16[576,1024]{1,0:T(8,128)(2,1)S(1)}, bf16[576,1024]{1,0:T(8,128)(2,1)}, u32[]{:S(2)}) copy-start(bf16[576,1024]{1,0:T(8,128)(2,1)} %param.20) | copy-start | bytes 3538948
  1.5 9.1 %copy-start.6 = (s32[2]{0:T(128)}, s32[2]{0:T(128)S(1)}, u32[]{:S(2)}) copy-start(s32[2]{0:T(128)S(1)} %dynamic_slice.9.own) | copy-start | bytes 28
  65.8 15.6 %copy-start.12 = (bf16[4,2,128,1024]{3,2,1,0:T(8,128)(2,1)S(1)}, bf16[4,2,128,1024]{3,2,1,0:T(8,128)(2,1)}, u32[]{:S(2)}) copy-start(bf16[4,2,128,1024]{3,2,1,0:T(8,128)(2,1)} %get-tuple-element.33) | copy-start | bytes 6291460
  81.5 47.6 %copy-start.10 = (bf16[1024,2,576]{0,2,1:T(8,128)(2,1)S(1)}, bf16[1024,2,576]{0,2,1:T(8,128)(2,1)}, u32[]{:S(2)}) copy-start(bf16[1024,2,576]{0,2,1:T(8,128)(2,1)} %param.19) | copy-start | bytes 7077892
  129.1 3.2 copy-start.13
  151.7 63.5 %copy-start.2 = (bf16[4,2,128,128]{3,2,1,0:T(8,128)(2,1)S(1)}, bf16[4,2,128,128]{3,2,1,0:T(8,128)(2,1)}, u32[]{:S(2)}) copy-start(bf16[4,2,128,128]{3,2,1,0:T(8,128)(2,1)} %get-tuple-element.36.attended) | copy-start | bytes 786436
  246.6 56.9 %copy-start.11 = (bf16[4,2,128,1024]{3,2,1,0:T(8,128)(2,1)S(1)}, bf16[4,2,128,1024]{3,2,1,0:T(8,128)(2,1)}, u32[]{:S(2)}) copy-start(bf16[4,2,128,1024]{3,2,1,0:T(8,128)(2,1)} %get-tuple-element.51) | copy-start | bytes 6291460
  306.2 60.3 %copy-start.9 = (f32[2,128]{1,0:T(2,128)S(1)}, f32[2,128]{1,0:T(2,128)}, u32[]{:S(2)}) copy-start(f32[2,128]{1,0:T(2,128)} %get-tuple-element.50) | copy-start | bytes 3076
  306.2 60.5 %copy-start.7 = (f32[1,1024]{1,0:T(1,128)S(1)}, f32[1,1024]{1,0:T(1,128)}, u32[]{:S(2)}) copy-start(f32[1,1024]{1,0:T(1,128)} %get-tuple-element.49) | copy-start | bytes 12292
  306.2 60.5 %copy-start.8 = (f32[1,1024]{1,0:T(1,128)S(1)}, f32[1,1024]{1,0:T(1,128)}, u32[]{:S(2)}) copy-start(f32[1,1024]{1,0:T(1,128)} %get-tuple-element.48) | copy-start | bytes 12292
  366.5 23.9 %copy-start.3 = (bf16[1,1024,384]{2,1,0:T(8,128)(2,1)S(1)}, bf16[1,1024,384]{2,1,0:T(8,128)(2,1)}, u32[]{:S(2)}) copy-start(bf16[1,1024,384]{2,1,0:T(8,128)(2,1)} %get-tuple-element.54) | copy-start | bytes 2359300
  404.1 5.8 %copy-start.4 = (bf16[4,2,16,1024]{3,2,1,0:T(8,128)(2,1)S(1)}, bf16[4,2,16,1024]{3,2,1,0:T(8,128)(2,1)}, u32[]{:S(2)}) copy-start(bf16[4,2,16,1024]{3,2,1,0:T(8,128)(2,1)} %get-tuple-element.109) | copy-start | bytes 786436
  404.1 6.5 %copy-start.5 = (bf16[4,2,16,1024]{3,2,1,0:T(8,128)(2,1)S(1)}, bf16[4,2,16,1024]{3,2,1,0:T(8,128)(2,1)}, u32[]{:S(2)}) copy-start(bf16[4,2,16,1024]{3,2,1,0:T(8,128)(2,1)} %get-tuple-element.110) | copy-start | bytes 786436
  404.1 7.3 %copy-start.1 = (bf16[576,1024]{1,0:T(8,128)(2,1)S(1)}, bf16[576,1024]{1,0:T(8,128)(2,1)}, u32[]{:S(2)}) copy-start(bf16[576,1024]{1,0:T(8,128)(2,1)} %param.20) | copy-start | bytes 3538948
